TPU v7x, 512 devices: a whole 4x4x16 slice. The times are simulated.
512 devices in a mesh: queue: 64 (over x, y, z_hi, core), head: 8 (over z_lo).
Axes of the slice: x: 4, y: 4, z: 16 (z_hi: 2, z_lo: 8; z = z_hi * 8 + z_lo), core: 2. Of those that a mesh axis runs over, the one named last changes fastest.
Arguments:
- projected: bfloat16 [32768, 3, 3072], P(('queue', 'head')), may hold values from -24 to 24
- prompt_states: bfloat16 [8, 2, 128, 3072], P(None, None, None, 'head'), may hold values from -24 to 24
- region_map: int32 [64, 512], P('queue'), may hold values from 0 to 3
- region_prompt: int32 [64, 4], P('queue'), may hold values from 0 to 7
- step_index: int32 [64], P('queue'), may hold values from 0 to 49
- time_gates: float32 [50, 3072], P(None, 'head'), may hold values from 0.1 to 1.9
- incoming: bfloat16 [512, 3072], P('head'), may hold values from -4 to 4
Outputs:
- advanced: bfloat16 [32768, 3072], P(('queue', 'head'))
All inputs are finite; a program needn't handle non-finite values.
Results may differ from a plain program's by a relative error of at most 0.003.
Values may be sent and summed in bfloat16 or wider, within the bound.
A program may use at most 64 MiB of HBM per device.

v0:
```python
import math

import jax
import jax.numpy as jnp
from jax import lax
from jax.sharding import PartitionSpec as P

HD = 128
L = 128
R = 4
NPROMPT = 8
NSTEPS = 50


NEG = -1e30


def padded(block, sides, width):
    for axis, dim in sides:
        count = lax.axis_size(axis)
        forward = [(i, i + 1) for i in range(count - 1)]
        backward = [(target, source) for source, target in forward]
        low = lax.ppermute(
            lax.slice_in_dim(block, block.shape[dim] - width, None, axis=dim), axis, forward
        )
        high = lax.ppermute(lax.slice_in_dim(block, 0, width, axis=dim), axis, backward)
        block = jnp.concatenate([low, block, high], axis=dim)
    return block


def from_behind(value, axis, steps):
    count = lax.axis_size(axis)
    first, last = (max(0, -steps), min(count, count - steps))
    return lax.ppermute(value, axis, [(source, source + steps) for source in range(first, last)])


def attend(queries, key_rows, value_rows, allowed):
    scores = jnp.dot(queries, key_rows.T, preferred_element_type=jnp.float32) * (
        1.0 / math.sqrt(HD)
    )
    scores = jnp.where(allowed, scores, NEG)
    highest = jnp.max(scores, axis=1, keepdims=True)
    weights = jnp.exp(scores - highest)
    totals = jnp.sum(weights, axis=1, keepdims=True)
    rounded = weights.astype(jnp.bfloat16)
    return jnp.dot(rounded, value_rows, preferred_element_type=jnp.float32) / totals


def per_device(
    projected, prompt_states, region_map, region_prompt, step_index, time_gates, incoming
):
    tok_rows = projected.shape[0]
    position = lax.axis_index("queue")
    chain_len = lax.axis_size("queue")
    rimmed = padded(projected[:, 1:3], (("queue", 0),), tok_rows)
    stacked = rimmed.reshape(3, tok_rows, 2, projected.shape[2])
    queries = lax.all_to_all(projected[:, 0], "head", split_axis=1, concat_axis=0, tiled=True)
    spread = lax.all_to_all(stacked, "head", split_axis=3, concat_axis=1, tiled=True)
    slab_rows = spread.shape[1]
    window = spread.reshape(3 * slab_rows, 2, spread.shape[3])
    channels = queries.shape[1]
    present = jnp.stack([position > 0, position >= 0, position < chain_len - 1])
    key_valid = jnp.repeat(present, slab_rows)
    selector = (region_prompt[0][:, None] == jnp.arange(NPROMPT, dtype=jnp.int32)[None, :]).astype(
        jnp.bfloat16
    )
    chosen = jnp.einsum(
        "rp,pxlc->xrlc", selector, prompt_states, preferred_element_type=jnp.float32
    )
    chosen = chosen.astype(jnp.bfloat16).reshape(2, R * L, channels)
    key_region = jnp.arange(R * L, dtype=jnp.int32) // L
    regions_here = region_map[0]
    block_rows = min(512, slab_rows)
    head_parts = []
    for head_idx in range(channels // HD):
        lower = head_idx * HD
        key_rows = window[:, 0, lower : lower + HD]
        value_rows = window[:, 1, lower : lower + HD]
        cross_keys = chosen[0, :, lower : lower + HD]
        cross_values = chosen[1, :, lower : lower + HD]
        query_block = queries[0:block_rows, lower : lower + HD]
        allowed_self = jnp.broadcast_to(key_valid[None, :], (block_rows, key_valid.shape[0]))
        allowed_cross = regions_here[0:block_rows, None] == key_region[None, :]
        self_out = attend(query_block, key_rows, value_rows, allowed_self)
        cross_out = attend(query_block, cross_keys, cross_values, allowed_cross)
        block_parts = self_out + cross_out
        head_parts.append(block_parts)
    summed = jnp.concatenate(head_parts, axis=1)
    picked = (jnp.arange(NSTEPS, dtype=jnp.int32) == step_index[0])[:, None]
    gate_row = jnp.sum(jnp.where(picked, time_gates, 0.0), axis=0)
    slab_out = (gate_row[None, :] * summed).astype(jnp.bfloat16)
    returned = lax.all_to_all(slab_out, "head", split_axis=0, concat_axis=1, tiled=True)
    moved = from_behind(returned, "queue", 1)
    return jnp.where(position == 0, incoming, moved)


def solution(mesh):
    return jax.shard_map(
        per_device,
        mesh=mesh,
        in_specs=(
            P(("queue", "head"), None, None),
            P(None, None, None, "head"),
            P("queue", None),
            P("queue", None),
            P("queue"),
            P(None, "head"),
            P("head", None),
        ),
        out_specs=P(("queue", "head"), None),
        check_vma=False,
    )
```

profile of v0, /device:TPU:34, one launch (start us, length us, event | category | flops | bytes accessed | tf_op | source)
XLA Modules:
  0.0 326.7 jit_solution(14558145350983736945)
XLA Ops:
  0.0 1.2 slice.53
  1.2 0.8 copy.28
  2.0 12.6 %all-to-all-start.1 = ((bf16[64,8,384]{2,0,1:T(8,128)(2,1)}), bf16[64,8,384]{2,0,1:T(8,128)(2,1)S(1)}, u32[]{:S(2)}, u32[]{:S(2)}) async-start(bf16[64,8,384]{2,0,1:T(8,128)(2,1)} %copy.28), calls=%async_computation.1 | async-start | bytes 786432 | tf_op jit(solution)/shard_map/all_to_all | solution.py:57
  14.7 9.5 %collective-permute-start.1 = (bf16[64,2,3072]{2,0,1:T(8,128)(2,1)S(1)}, bf16[64,2,3072]{2,0,1:T(8,128)(2,1)S(1)}, u32[]{:S(2)}, u32[]{:S(2)}) collective-permute-start(bf16[64,2,3072]{2,0,1:T(8,128)(2,1)S(1)} %slice.51), channel_id=1, source_target_pairs={{8,0},{16,8},{24,16},{32,24},{40,32},{48,40},{56,48},{64,56},{72,6... | collective-permute-start | bytes 2359304 | tf_op jit(solution)/shard_map/ppermute | solution.py:26
  24.3 1.9 collective-permute-start
  26.2 21.1 %collective-permute-done.1 = bf16[64,2,3072]{2,0,1:T(8,128)(2,1)S(1)} collective-permute-done((bf16[64,2,3072]{2,0,1:T(8,128)(2,1)S(1)}, bf16[64,2,3072]{2,0,1:T(8,128)(2,1)S(1)}, u32[]{:S(2)}, u32[]{:S(2)}) %collective-permute-start.1) | collective-permute-done | bytes 786464 | tf_op jit(solution)/shard_map/ppermute | solution.py:26
  47.3 5.2 %collective-permute-done = bf16[64,2,3072]{2,0,1:T(8,128)(2,1)S(1)} collective-permute-done((bf16[64,2,3072]{2,0,1:T(8,128)(2,1)S(1)}, bf16[64,2,3072]{2,0,1:T(8,128)(2,1)S(1)}, u32[]{:S(2)}, u32[]{:S(2)}) %collective-permute-start) | collective-permute-done | bytes 786464 | tf_op jit(solution)/shard_map/ppermute | solution.py:23
  52.5 1.6 pad_maximum_fusion
  54.1 10.8 %copy.25 = bf16[3,64,2,3072]{1,2,0,3:T(2,128)(2,1)} copy(bf16[3,64,2,3072]{3,1,0,2:T(8,128)(2,1)} %bitcast.98) | data formatting | bytes 4718592 | tf_op jit(solution)/shard_map/reshape | solution.py:56
  65.0 7.9 %reshape.62 = bf16[8,2,73728]{2,1,0:T(2,128)(2,1)} reshape(bf16[3072,3,2,64]{3,2,1,0:T(2,128)(2,1)} %bitcast.96) | data formatting | bytes 4718592
  72.9 11.3 %all-to-all-done.1 = bf16[64,8,384]{2,0,1:T(8,128)(2,1)S(1)} async-done(((bf16[64,8,384]{2,0,1:T(8,128)(2,1)}), bf16[64,8,384]{2,0,1:T(8,128)(2,1)S(1)}, u32[]{:S(2)}, u32[]{:S(2)}) %all-to-all-start.1) | async-done | bytes 393248 | tf_op jit(solution)/shard_map/all_to_all | solution.py:57
  84.2 50.1 %all-to-all-start = ((bf16[8,2,73728]{2,1,0:T(2,128)(2,1)}), bf16[8,2,73728]{2,1,0:T(2,128)(2,1)}, u32[]{:S(2)}, u32[]{:S(2)}) async-start(bf16[8,2,73728]{2,1,0:T(2,128)(2,1)} %reshape.62), calls=%async_computation | async-start | bytes 4718592 | tf_op jit(solution)/shard_map/all_to_all | solution.py:58
  135.1 1.1 fusion.26
  138.1 0.3 convolution_divide_fusion
  138.4 0.3 convolution_divide_fusion.1
  138.8 0.3 convolution_divide_fusion.2
  139.1 96.3 %all-to-all-done = bf16[8,2,73728]{2,1,0:T(2,128)(2,1)} async-done(((bf16[8,2,73728]{2,1,0:T(2,128)(2,1)}), bf16[8,2,73728]{2,1,0:T(2,128)(2,1)}, u32[]{:S(2)}, u32[]{:S(2)}) %all-to-all-start) | async-done | bytes 2359328 | tf_op jit(solution)/shard_map/all_to_all | solution.py:58
  235.5 7.7 %reshape.63 = bf16[3072,3,2,64]{3,2,1,0:T(2,128)(2,1)} reshape(bf16[8,2,73728]{2,1,0:T(2,128)(2,1)} %all-to-all-done) | data formatting | bytes 4718592
  243.1 11.9 %copy.34 = bf16[3,64,2,8,384]{4,1,3,0,2:T(8,128)(2,1)} copy(bf16[3,64,2,8,384]{1,2,0,4,3:T(2,128)(2,1)} %bitcast.97) | data formatting | bytes 4718592 | tf_op jit(solution)/shard_map/all_to_all | solution.py:58
  255.0 1.7 fusion.73
  256.8 0.6 fusion.75
  257.4 0.6 fusion.77
  258.0 0.5 fusion.7
  258.5 0.6 fusion.44
  259.1 0.5 fusion.5
  259.6 0.6 fusion.38
  260.2 0.5 fusion.3
  260.7 0.6 fusion.32
  261.4 31.2 %all_to_all.50 = bf16[8,64,384]{2,1,0:T(8,128)(2,1)S(1)} all-to-all(bf16[8,64,384]{2,1,0:T(8,128)(2,1)S(1)} %fusion.53), channel_id=1, replica_groups=mesh['queue'=64,'head'=8] {'head'}, dimensions={0} | all-to-all | bytes 786432 | tf_op jit(solution)/shard_map/all_to_all | solution.py:92
  292.7 1.9 collective-permute-start.2
  294.6 31.2 %collective-permute-done.2 = bf16[64,3072]{1,0:T(8,128)(2,1)S(1)} collective-permute-done((bf16[64,3072]{1,0:T(8,128)(2,1)S(1)}, bf16[64,3072]{1,0:T(8,128)(2,1)S(1)}, u32[]{:S(2)}, u32[]{:S(2)}) %collective-permute-start.2) | collective-permute-done | bytes 393248 | tf_op jit(solution)/shard_map/ppermute | solution.py:34
  325.9 0.8 broadcast_select_fusion
  (31 shorter events, 2.2 us)
Async XLA Ops:
  0.0 135.1 %copy-start = (bf16[8,2,128,384]{3,2,1,0:T(8,128)(2,1)S(1)}, bf16[8,2,128,384]{3,2,1,0:T(8,128)(2,1)}, u32[]{:S(2)}) copy-start(bf16[8,2,128,384]{3,2,1,0:T(8,128)(2,1)} %param.8) | copy-start | bytes 4718596
  0.0 14.7 %copy-start.2 = (bf16[64,3,3072]{2,0,1:T(8,128)(2,1)S(1)}, bf16[64,3,3072]{2,0,1:T(8,128)(2,1)}, u32[]{:S(2)}) copy-start(bf16[64,3,3072]{2,0,1:T(8,128)(2,1)} %param.7) | copy-start | bytes 3538948
  2.0 82.1 %all-to-all-start.1 = ((bf16[64,8,384]{2,0,1:T(8,128)(2,1)}), bf16[64,8,384]{2,0,1:T(8,128)(2,1)S(1)}, u32[]{:S(2)}, u32[]{:S(2)}) async-start(bf16[64,8,384]{2,0,1:T(8,128)(2,1)} %copy.28), calls=%async_computation.1 | async-start | bytes 786432 | tf_op jit(solution)/shard_map/all_to_all | solution.py:57
  14.7 32.6 %collective-permute-start.1 = (bf16[64,2,3072]{2,0,1:T(8,128)(2,1)S(1)}, bf16[64,2,3072]{2,0,1:T(8,128)(2,1)S(1)}, u32[]{:S(2)}, u32[]{:S(2)}) collective-permute-start(bf16[64,2,3072]{2,0,1:T(8,128)(2,1)S(1)} %slice.51), channel_id=1, source_target_pairs={{8,0},{16,8},{24,16},{32,24},{40,32},{48,40},{56,48},{64,56},{72,6... | collective-permute-start | bytes 2359304 | tf_op jit(solution)/shard_map/ppermute | solution.py:26
  24.3 28.3 %collective-permute-start = (bf16[64,2,3072]{2,0,1:T(8,128)(2,1)S(1)}, bf16[64,2,3072]{2,0,1:T(8,128)(2,1)S(1)}, u32[]{:S(2)}, u32[]{:S(2)}) collective-permute-start(bf16[64,2,3072]{2,0,1:T(8,128)(2,1)S(1)} %slice.51), channel_id=1, source_target_pairs={{0,8},{8,16},{16,24},{24,32},{32,40},{40,48},{48,56},{56,64},{64,7... | collective-permute-start | bytes 2359304 | tf_op jit(solution)/shard_map/ppermute | solution.py:23
  72.9 62.2 %copy-start.5 = (s32[1,4]{1,0:T(1,128)S(1)}, s32[1,4]{1,0:T(1,128)}, u32[]{:S(2)}) copy-start(s32[1,4]{1,0:T(1,128)} %param.10) | copy-start | bytes 52
  84.2 151.3 %all-to-all-start = ((bf16[8,2,73728]{2,1,0:T(2,128)(2,1)}), bf16[8,2,73728]{2,1,0:T(2,128)(2,1)}, u32[]{:S(2)}, u32[]{:S(2)}) async-start(bf16[8,2,73728]{2,1,0:T(2,128)(2,1)} %reshape.62), calls=%async_computation | async-start | bytes 4718592 | tf_op jit(solution)/shard_map/all_to_all | solution.py:58
  134.3 2.1 copy-start.4
  134.3 2.2 copy-start.6
  255.0 1.8 copy-start.1
  260.7 65.1 %copy-start.3 = (bf16[64,3072]{1,0:T(8,128)(2,1)S(1)}, bf16[64,3072]{1,0:T(8,128)(2,1)}, u32[]{:S(2)}) copy-start(bf16[64,3072]{1,0:T(8,128)(2,1)} %param.13) | copy-start | bytes 1179652
  292.7 33.2 %collective-permute-start.2 = (bf16[64,3072]{1,0:T(8,128)(2,1)S(1)}, bf16[64,3072]{1,0:T(8,128)(2,1)S(1)}, u32[]{:S(2)}, u32[]{:S(2)}) collective-permute-start(bf16[64,3072]{1,0:T(8,128)(2,1)S(1)} %bitcast.123), channel_id=1, source_target_pairs={{0,8},{8,16},{16,24},{24,32},{32,40},{40,48},{48,56},{56,64},{64,7... | collective-permute-start | bytes 1179656 | tf_op jit(solution)/shard_map/ppermute | solution.py:34
where the time goes:
time: 328 us; the launch traced here: 327 us
  waiting for transfers between devices  165 us (50%)
  starting transfers between devices  76.1 us (23%)
  local copies, waits for them, and re-layouts  40.7 us (12%)
  blocking collectives  31.2 us (10%)
  matrix products  7.87 us (2%)
  other arithmetic  4.72 us (1%)
    all_to_all x1, waiting for transfers between devices, per_device(): lax.all_to_all(stacked, 'head', split_axis=3, concat_axis=1, tiled=True)  96.3 us
    all_to_all x1, starting transfers between devices, per_device(): lax.all_to_all(stacked, 'head', split_axis=3, concat_axis=1, tiled=True)  50.1 us
    all_to_all x1, blocking collectives, per_device(): lax.all_to_all(slab_out, 'head', split_axis=0, concat_axis=1, tiled=True)  31.2 us
    ppermute x1, waiting for transfers between devices, from_behind(): lax.ppermute(value, axis, [(source, source + steps) for source in range(f...  31.2 us
    ppermute x1, waiting for transfers between devices, padded(): lax.ppermute(lax.slice_in_dim(block, 0, width, axis=dim), axis, backward)  21.1 us
    unnamed x17, local copies, waits for them, and re-layouts  15.7 us
    all_to_all x1, starting transfers between devices, per_device(): lax.all_to_all(projected[:, 0], 'head', split_axis=1, concat_axis=0, tile...  12.6 us
    all_to_all x1, local copies, waits for them, and re-layouts, per_device(): lax.all_to_all(stacked, 'head', split_axis=3, concat_axis=1, tiled=True)  11.9 us
  transfers between devices with their start and end apart: 5, of which 5 were waited for; matrix products, arithmetic and copies ran while one was open for 7% of the time, Pallas kernels for 0%

commit v1 on v0

v1 whole, which is shorter than its diff:
```python
import math

import jax
import jax.numpy as jnp
from jax import lax
from jax.experimental import pallas as pl
from jax.experimental.pallas import tpu as pltpu
from jax.sharding import PartitionSpec as P

HD = 128
L = 128
R = 4
NPROMPT = 8
GROUP = 4
PER = 3

NEG = -1e30
FAR = 1e30
SCALE = math.log2(math.e) / math.sqrt(HD)
MESH = pl.DeviceIdType.MESH


def worker_of(z, hl):
    free = lax.rem(z, 2) * 2 + 1
    return hl + jnp.where(hl >= free, 1, 0)


def attention_kernel(
    nq, nz,
    proj, prompts, rmap, rprompt, step, gates,
    out,
    kv, qb, ob, pkv, rmap_v, gates_v, meta_src, meta,
    kv_sem, q_sem, halo_sem, meta_sem, out_sem, local_sem,
    send_sem, halo_send, meta_send, out_send,
):
    rows = proj.shape[1]
    slab = rows * nz
    half = slab // 2
    heads = PER * nz
    q = lax.axis_index("queue")
    j = lax.axis_index("head")
    c = lax.div(q, GROUP)
    a = lax.rem(q, GROUP)
    free = lax.rem(j, 2) * 2 + 1
    works = a != free
    hl = a - jnp.where(a > free, 1, 0)
    right = lax.rem(q + GROUP, nq)
    left = lax.rem(q + nq - GROUP, nq)
    place = a * nz + j
    members = GROUP * nz

    barrier = pltpu.get_barrier_semaphore()

    def greet(i, carry):
        other = lax.rem(place + i, members)
        pl.semaphore_signal(
            barrier, inc=1,
            device_id={"queue": c * GROUP + lax.div(other, nz), "head": lax.rem(other, nz)},
            device_id_type=MESH,
        )
        return carry

    lax.fori_loop(1, members, greet, 0)
    for side in (left, right):
        pl.semaphore_signal(
            barrier, inc=1, device_id={"queue": side, "head": j}, device_id_type=MESH
        )
    map_copy = pltpu.make_async_copy(rmap, rmap_v, local_sem.at[0])
    gate_copy = pltpu.make_async_copy(gates, gates_v, local_sem.at[1])
    lane = pl.multiple_of(jnp.minimum(hl, PER - 1) * HD, HD)
    prompt_copy = pltpu.make_async_copy(
        prompts.at[:, :, :, pl.ds(lane, HD)], pkv, local_sem.at[2]
    )
    map_copy.start()
    gate_copy.start()
    prompt_copy.start()
    pl.semaphore_wait(barrier, members + 1)

    def spread(first, last, dst, sem):
        def body(n, carry):
            z2 = lax.rem(j + lax.div(n, PER), nz)
            hl2 = lax.rem(n, PER)
            a2 = worker_of(z2, hl2)
            col = pl.multiple_of((z2 * PER + hl2) * HD, HD)
            src = proj.at[first:last, :, pl.ds(col, HD)]
            mine = (a2 == a) & (z2 == j)

            @pl.when(mine)
            def _():
                pltpu.make_async_copy(src, dst, sem).start()

            @pl.when(jnp.logical_not(mine))
            def _():
                pltpu.make_async_remote_copy(
                    src_ref=src, dst_ref=dst, send_sem=send_sem, recv_sem=sem,
                    device_id={"queue": c * GROUP + a2, "head": z2}, device_id_type=MESH,
                ).start()

            return carry

        lax.fori_loop(0, heads, body, 0)

    kv_row = pl.multiple_of((a + 1) * slab + j * rows, rows)
    spread(1, 3, kv.at[:, pl.ds(kv_row, rows), :], kv_sem.at[a])

    map_copy.wait()
    gate_copy.wait()
    regions = rmap_v[...]
    token_prompt = jnp.zeros(regions.shape, jnp.int32)
    for r in range(R):
        token_prompt = jnp.where(regions == r, rprompt[0, r], token_prompt)
    token_prompt = token_prompt.astype(jnp.float32)
    for i in range(slab // 128):
        meta_src[i : i + 1, :] = token_prompt[:, i * 128 : (i + 1) * 128]
    table = gates_v[...]
    picked = lax.broadcasted_iota(jnp.int32, table.shape, 0) == step[0]
    gate_row = jnp.sum(jnp.where(picked, table, 0.0), axis=0, keepdims=True)
    for i in range(PER):
        meta_src[4 + i : 5 + i, :] = gate_row[:, i * HD : (i + 1) * HD]
    meta_src[7:8, :] = jnp.zeros((1, 128), jnp.float32)
    pltpu.make_async_copy(meta_src, meta.at[a], meta_sem).start()
    for i in range(1, GROUP):
        pltpu.make_async_remote_copy(
            src_ref=meta_src, dst_ref=meta.at[a], send_sem=meta_send.at[i - 1], recv_sem=meta_sem,
            device_id={"queue": c * GROUP + lax.rem(a + i, GROUP), "head": j},
            device_id_type=MESH,
        ).start()

    q_row = pl.multiple_of(a * slab + j * rows, rows)
    part = lax.div(j, nz // 2)
    spread(0, 1, qb.at[:, pl.ds(q_row, rows), :], q_sem.at[a * 2 + part])

    def wait_for(ref, sem):
        pltpu.make_async_copy(ref, ref, sem).wait()

    wait_for(meta, meta_sem)
    prompt_copy.wait()

    @pl.when(works)
    def _():
        for s in range(GROUP):
            wait_for(kv.at[:, (s + 1) * slab : (s + 2) * slab, :], kv_sem.at[s])
        halos = (
            (1, GROUP + 1, left, 0),
            (GROUP, 0, right, 1),
        )
        copies = [
            pltpu.make_async_remote_copy(
                src_ref=kv.at[:, src * slab : (src + 1) * slab, :],
                dst_ref=kv.at[:, dst * slab : (dst + 1) * slab, :],
                send_sem=halo_send.at[k], recv_sem=halo_sem.at[k],
                device_id={"queue": side, "head": j}, device_id_type=MESH,
            )
            for src, dst, side, k in halos
        ]
        for copy in copies:
            copy.start()
        head_col = pl.multiple_of((j * PER + hl) * HD, HD)
        pk = [pkv.at[p, 0] for p in range(NPROMPT)]
        ones = jnp.ones((3 * slab, HD), jnp.bfloat16)

        def one_slab(t, carry):
            s = lax.rem(t + 1, GROUP)

            @pl.when(t == 2)
            def _():
                copies[0].wait_recv()

            @pl.when(t == 3)
            def _():
                copies[1].wait_recv()

            left_ok = (c > 0) | (s > 0)
            right_ok = (c < nq // GROUP - 1) | (s < GROUP - 1)
            here = meta[s]
            gate = jnp.where(
                hl == 0, here[4:5, :], jnp.where(hl == 1, here[5:6, :], here[6:7, :])
            )
            for part in range(2):
                row = pl.multiple_of(s * slab + part * half, half)
                wait_for(qb.at[:, pl.ds(row, half), :], q_sem.at[s * 2 + part])
                qv = qb[0, pl.ds(row, half), :]
                first = pl.multiple_of(s * slab, slab)
                keys = kv[0, pl.ds(first, 3 * slab), :]
                values = kv[1, pl.ds(first, 3 * slab), :]
                scores = lax.dot_general(
                    qv, keys, (((1,), (1,)), ((), ())), preferred_element_type=jnp.float32
                )
                parts = [scores[:, i * slab : (i + 1) * slab] for i in range(3)]
                tops = [jnp.max(x, axis=1, keepdims=True) for x in parts]
                top = jnp.maximum(
                    tops[1],
                    jnp.maximum(jnp.where(left_ok, tops[0], NEG), jnp.where(right_ok, tops[2], NEG)),
                )
                shifts = (jnp.where(left_ok, top, FAR), top, jnp.where(right_ok, top, FAR))
                probs = jnp.concatenate(
                    [jnp.exp2((x - y) * SCALE).astype(jnp.bfloat16) for x, y in zip(parts, shifts)],
                    axis=1,
                )
                both = jnp.dot(
                    probs, jnp.concatenate([values, ones], axis=1),
                    preferred_element_type=jnp.float32,
                )
                result = both[:, :HD] / both[:, HD:]

                chosen = jnp.concatenate(
                    [
                        jnp.broadcast_to(here[i : i + 1, :], (128, 128)).T
                        for i in range(part * half // 128, (part + 1) * half // 128)
                    ],
                    axis=0,
                )
                cross = jnp.zeros((half, L), jnp.float32)
                for p in range(NPROMPT):
                    one = lax.dot_general(
                        qv, pk[p][...], (((1,), (1,)), ((), ())),
                        preferred_element_type=jnp.float32,
                    )
                    cross = jnp.where(chosen == float(p), one, cross)
                cross_top = jnp.max(cross, axis=1, keepdims=True)
                weights = jnp.exp2((cross - cross_top) * SCALE)
                total = jnp.sum(weights, axis=1, keepdims=True)
                masked = jnp.concatenate(
                    [
                        jnp.where(chosen == float(p), weights, 0.0).astype(jnp.bfloat16)
                        for p in range(NPROMPT)
                    ],
                    axis=1,
                )
                stacked = jnp.concatenate([pkv[p, 1] for p in range(NPROMPT)], axis=0)
                result = result + jnp.dot(
                    masked, stacked, preferred_element_type=jnp.float32
                ) / total
                ob[pl.ds(row, half), :] = (gate * result).astype(jnp.bfloat16)

                target = lax.rem(c * GROUP + s + 1, nq)
                for i in range(nz // 2):
                    z2 = part * (nz // 2) + i
                    src = ob.at[pl.ds(pl.multiple_of(row + i * rows, rows), rows), :]
                    dst = out.at[:, pl.ds(head_col, HD)]
                    mine = (target == q) & (j == z2)

                    @pl.when(mine)
                    def _():
                        pltpu.make_async_copy(src, dst, out_sem).start()

                    @pl.when(jnp.logical_not(mine))
                    def _():
                        pltpu.make_async_remote_copy(
                            src_ref=src, dst_ref=dst, send_sem=out_send, recv_sem=out_sem,
                            device_id={"queue": target, "head": z2}, device_id_type=MESH,
                        ).start()

            return carry

        lax.fori_loop(0, GROUP, one_slab, 0)
        for copy in copies:
            copy.wait_send()
        wait_for(proj.at[:, :, : (heads - 1) * HD], send_sem)

        @pl.when(a == 0)
        def _():
            wait_for(ob, out_send)

        @pl.when(a > 0)
        def _():
            wait_for(ob.at[: GROUP * slab - rows, :], out_send)

    @pl.when(jnp.logical_not(works))
    def _():
        wait_for(proj, send_sem)

    for i in range(GROUP - 1):
        wait_for(meta_src, meta_send.at[i])
    wait_for(out, out_sem)


def solution(mesh):
    nq, nz = mesh.shape["queue"], mesh.shape["head"]

    def per_device(
        projected, prompt_states, region_map, region_prompt, step_index, time_gates, incoming
    ):
        rows, _, channels = projected.shape
        slab = rows * nz
        anywhere = pl.BlockSpec(memory_space=pl.ANY)
        scalars = pl.BlockSpec(memory_space=pltpu.SMEM)
        dma = pltpu.SemaphoreType.DMA

        def kernel(*refs):
            attention_kernel(nq, nz, *refs)

        moved = pl.pallas_call(
            kernel,
            out_shape=jax.ShapeDtypeStruct((rows, channels), jnp.bfloat16),
            in_specs=[anywhere, anywhere, anywhere, scalars, scalars, anywhere],
            out_specs=anywhere,
            scratch_shapes=[
                pltpu.VMEM((2, (GROUP + 2) * slab, HD), jnp.bfloat16),
                pltpu.VMEM((1, GROUP * slab, HD), jnp.bfloat16),
                pltpu.VMEM((GROUP * slab, HD), jnp.bfloat16),
                pltpu.VMEM((NPROMPT, 2, L, HD), jnp.bfloat16),
                pltpu.VMEM(region_map.shape, jnp.int32),
                pltpu.VMEM(time_gates.shape, jnp.float32),
                pltpu.VMEM((8, 128), jnp.float32),
                pltpu.VMEM((GROUP, 8, 128), jnp.float32),
                dma((GROUP,)),
                dma((2 * GROUP,)),
                dma((2,)),
                dma,
                dma,
                dma((3,)),
                dma,
                dma((2,)),
                dma((GROUP - 1,)),
                dma,
            ],
            compiler_params=pltpu.CompilerParams(
                collective_id=0, has_side_effects=True, vmem_limit_bytes=48 * 1024 * 1024
            ),
        )(
            projected.transpose(1, 0, 2), prompt_states, region_map, region_prompt, step_index,
            time_gates,
        )
        return jnp.where(lax.axis_index("queue") == 0, incoming, moved)

    return jax.shard_map(
        per_device,
        mesh=mesh,
        in_specs=(
            P(("queue", "head"), None, None),
            P(None, None, None, "head"),
            P("queue", None),
            P("queue", None),
            P("queue"),
            P(None, "head"),
            P("head", None),
        ),
        out_specs=P(("queue", "head"), None),
        check_vma=False,
    )
```

time: 328 us -> 113 us (0.34)
  the two profiles are of different devices: /device:TPU:34 before, /device:TPU:1 now
where the time goes in v1:
time: 113 us
  Pallas kernels  106 us (94%)
  local copies, waits for them, and re-layouts  4.9 us (4%)
    pallas_call x1, Pallas kernels, per_device(): pl.pallas_call(kernel, out_shape=jax.ShapeDtypeStruct((rows, channels), j...  106 us
    unnamed x12, local copies, waits for them, and re-layouts  4.9 us

profile of v1, /device:TPU:1, one launch (start us, length us, event | category | flops | bytes accessed | tf_op | source)
XLA Modules:
  0.0 112.6 jit_solution(14407289101547984040)
XLA Ops:
  0.7 0.0 copy-start
  0.7 1.4 %copy-done = bf16[8,2,128,384]{3,2,1,0:T(8,128)(2,1)S(1)} copy-done((bf16[8,2,128,384]{3,2,1,0:T(8,128)(2,1)S(1)}, bf16[8,2,128,384]{3,2,1,0:T(8,128)(2,1)}, u32[]{:S(2)}) %copy-start) | copy-done | bytes 1572888
  2.1 0.0 copy-start.1
  2.1 1.3 %copy-done.1 = bf16[64,3,3072]{2,0,1:T(8,128)(2,1)S(1)} copy-done((bf16[64,3,3072]{2,0,1:T(8,128)(2,1)S(1)}, bf16[64,3,3072]{2,0,1:T(8,128)(2,1)}, u32[]{:S(2)}) %copy-start.1) | copy-done | bytes 1179672
  3.3 0.0 copy-start.2
  3.3 0.9 copy-done.2
  4.2 0.0 copy-start.3
  4.2 0.7 copy-done.3
  4.9 0.0 copy-start.4
  4.9 0.7 copy-done.4
  5.6 0.0 copy-start.5
  5.6 106.2 %shard_map.73 = bf16[64,3072]{1,0:T(8,128)(2,1)S(1)} custom-call(bf16[3,64,3072]{2,1,0:T(8,128)(2,1)S(1)} %bitcast.1, bf16[8,2,128,384]{3,2,1,0:T(8,128)(2,1)S(1)} %copy-done, s32[1,512]{1,0:T(1,128)S(1)} %copy-done.3, s32[1,4]{1,0:T(1,128)S(1)} %copy-done.4, s32[1]{0:T(128)S(6)} %copy.8.refs_4_, f32[50,384]{1,0:T(8,128)S(1)} %copy-done.2), custom_call_target="tpu_custom_call" | custom-call | tf_op jit(solution)/shard_map/pallas_call | solution.py:293
  111.8 0.0 copy-done.5
  111.8 0.8 broadcast_select_fusion
Async XLA Ops:
  0.7 1.4 %copy-start = (bf16[8,2,128,384]{3,2,1,0:T(8,128)(2,1)S(1)}, bf16[8,2,128,384]{3,2,1,0:T(8,128)(2,1)}, u32[]{:S(2)}) copy-start(bf16[8,2,128,384]{3,2,1,0:T(8,128)(2,1)} %refs_1_.1) | copy-start | bytes 4718596
  2.1 1.3 %copy-start.1 = (bf16[64,3,3072]{2,0,1:T(8,128)(2,1)S(1)}, bf16[64,3,3072]{2,0,1:T(8,128)(2,1)}, u32[]{:S(2)}) copy-start(bf16[64,3,3072]{2,0,1:T(8,128)(2,1)} %param.7) | copy-start | bytes 3538948
  3.3 0.9 copy-start.2
  4.2 0.7 copy-start.3
  4.9 0.7 copy-start.4
  5.6 106.2 %copy-start.5 = (bf16[64,3072]{1,0:T(8,128)(2,1)S(1)}, bf16[64,3072]{1,0:T(8,128)(2,1)}, u32[]{:S(2)}) copy-start(bf16[64,3072]{1,0:T(8,128)(2,1)} %param.13) | copy-start | bytes 1179652

commit v2 on v1

v2 whole, which is shorter than its diff:
```python
import math

import jax
import jax.numpy as jnp
from jax import lax
from jax.experimental import pallas as pl
from jax.experimental.pallas import tpu as pltpu
from jax.sharding import PartitionSpec as P

HD = 128
L = 128
R = 4
NPROMPT = 8
GROUP = 4
PER = 3

NEG = -1e30
FAR = 1e30
SCALE = math.log2(math.e) / math.sqrt(HD)
THROTTLE = False
FARKV = True
FARQ = False
MESH = pl.DeviceIdType.MESH


def free_place(z):
    upper = (z == 1) | (z == 2) | (z == 4) | (z == 7)
    return jnp.where(upper, 3, 1)


def wrapped(value, count):
    return jnp.where(value >= count, value - count, jnp.where(value < 0, value + count, value))


def wait_for(ref, sem):
    pltpu.make_async_copy(ref, ref, sem).wait()


def attention_kernel(
    nq, nz,
    proj, prompts, rmap, rprompt, step, gates,
    out,
    kv, qb, ob, pkv, rmap_v, gates_v, meta_src, meta,
    edge_sem, kv_sem, q_sem, halo_sem, meta_sem, out_sem, local_sem,
    kv_send, q_send, halo_send, meta_send, out_send,
):
    rows = proj.shape[1]
    slab = rows * nz
    half = slab // 2
    heads = PER * nz
    ring = 2 * nz
    q = lax.axis_index("queue")
    j = lax.axis_index("head")
    c = lax.div(q, GROUP)
    base = c * GROUP
    a = q - base
    arc = jnp.where(a >= 2, 1, 0)
    core = a - 2 * arc
    z = arc * nz + j
    free = free_place(j)
    works = a != free
    hl = a - jnp.where(a > free, 1, 0)
    right = wrapped(q + GROUP, nq)
    left = wrapped(q - GROUP, nq)

    barrier = pltpu.get_barrier_semaphore()

    def greet(chip, k):
        upper = jnp.where(chip >= nz, 1, 0)
        pl.semaphore_signal(
            barrier, inc=1,
            device_id={"queue": base + 2 * upper + k, "head": chip - nz * upper},
            device_id_type=MESH,
        )

    def greet_chip(m, carry):
        chip = wrapped(z + m, ring)
        greet(chip, 0)
        greet(chip, 1)
        return carry

    lax.fori_loop(1, ring, greet_chip, 0)
    greet(z, 1 - core)
    for side in (left, right):
        pl.semaphore_signal(
            barrier, inc=1, device_id={"queue": side, "head": j}, device_id_type=MESH
        )
    map_copy = pltpu.make_async_copy(rmap, rmap_v, local_sem.at[0])
    gate_copy = pltpu.make_async_copy(gates, gates_v, local_sem.at[1])
    lane = pl.multiple_of(jnp.minimum(hl, PER - 1) * HD, HD)
    prompt_copy = pltpu.make_async_copy(
        prompts.at[:, :, :, pl.ds(lane, HD)], pkv, local_sem.at[2]
    )
    map_copy.start()
    gate_copy.start()
    prompt_copy.start()
    pl.semaphore_wait(barrier, 2 * ring + 1)

    def spread(first, last, dst, send_sem, recv_sem, far):
        def piece(chip, k):
            upper = jnp.where(chip >= nz, 1, 0)
            z2 = chip - nz * upper
            a2 = 2 * upper + k
            free2 = free_place(z2)
            hl2 = a2 - jnp.where(a2 > free2, 1, 0)
            col = pl.multiple_of((z2 * PER + jnp.minimum(hl2, PER - 1)) * HD, HD)
            return a2 != free2, base + a2, z2, proj.at[first:last, :, pl.ds(col, HD)]

        def send(chip, k):
            real, q2, z2, src = piece(chip, k)

            def go():
                pltpu.make_async_remote_copy(
                    src_ref=src, dst_ref=dst, send_sem=send_sem, recv_sem=recv_sem,
                    device_id={"queue": q2, "head": z2}, device_id_type=MESH,
                ).start()

            if k == 0:
                go()
            else:
                pl.when(real)(go)

        def both_ways(m, carry):
            d = nz - m if far else m
            for off in (d, -d):
                chip = wrapped(z + off, ring)
                send(chip, 0)
                send(chip, 1)
            return carry

        @pl.when(works)
        def _():
            pltpu.make_async_copy(piece(z, core)[3], dst, recv_sem).start()

        for k in range(2):
            @pl.when((core != k) & ((k == 0) | (2 * arc + 1 != free)))
            def _():
                real, q2, z2, src = piece(z, k)
                pltpu.make_async_remote_copy(
                    src_ref=src, dst_ref=dst, send_sem=send_sem, recv_sem=recv_sem,
                    device_id={"queue": q2, "head": z2}, device_id_type=MESH,
                ).start()

        opposite = wrapped(z + nz, ring)
        if far:
            send(opposite, 0)
            send(opposite, 1)
        lax.fori_loop(1, nz, both_ways, 0)
        if not far:
            send(opposite, 0)
            send(opposite, 1)

    def sent(first, last, sem):
        @pl.when(works)
        def _():
            wait_for(proj.at[first:last, :, : (heads - 1) * HD], sem)

        @pl.when(jnp.logical_not(works))
        def _():
            wait_for(proj.at[first:last], sem)

    kv_row = pl.multiple_of((a + 1) * slab + j * rows, rows)
    kv_dst = kv.at[:, pl.ds(kv_row, rows), :]
    at_edge = (a == 0) | (a == GROUP - 1)

    @pl.when(at_edge)
    def _():
        spread(1, 3, kv_dst, kv_send, edge_sem.at[jnp.where(a == 0, 0, 1), j], FARKV)

    @pl.when(jnp.logical_not(at_edge))
    def _():
        spread(1, 3, kv_dst, kv_send, kv_sem.at[core], FARKV)

    map_copy.wait()
    gate_copy.wait()
    regions = rmap_v[...]
    token_prompt = jnp.zeros(regions.shape, jnp.int32)
    for r in range(R):
        token_prompt = jnp.where(regions == r, rprompt[0, r], token_prompt)
    token_prompt = token_prompt.astype(jnp.float32)
    for i in range(slab // 128):
        meta_src[i : i + 1, :] = token_prompt[:, i * 128 : (i + 1) * 128]
    table = gates_v[...]
    picked = lax.broadcasted_iota(jnp.int32, table.shape, 0) == step[0]
    gate_row = jnp.sum(jnp.where(picked, table, 0.0), axis=0, keepdims=True)
    for i in range(PER):
        meta_src[4 + i : 5 + i, :] = gate_row[:, i * HD : (i + 1) * HD]
    meta_src[7:8, :] = jnp.zeros((1, 128), jnp.float32)
    pltpu.make_async_copy(meta_src, meta.at[a], meta_sem).start()
    for i in range(1, GROUP):
        pltpu.make_async_remote_copy(
            src_ref=meta_src, dst_ref=meta.at[a], send_sem=meta_send.at[i - 1], recv_sem=meta_sem,
            device_id={"queue": base + wrapped(a + i, GROUP), "head": j},
            device_id_type=MESH,
        ).start()

    if THROTTLE:
        sent(1, 3, kv_send)
    q_row = pl.multiple_of(a * slab + j * rows, rows)
    spread(
        0, 1, qb.at[:, pl.ds(q_row, rows), :], q_send,
        q_sem.at[a * 2 + jnp.where(j >= nz // 2, 1, 0)], FARQ,
    )

    @pl.when(works)
    def _():
        def halo(side, n):
            src, dst, to = ((1, GROUP + 1, left), (GROUP, 0, right))[side]
            return pltpu.make_async_remote_copy(
                src_ref=kv.at[:, pl.ds(pl.multiple_of(src * slab + n * rows, rows), rows), :],
                dst_ref=kv.at[:, pl.ds(pl.multiple_of(dst * slab + n * rows, rows), rows), :],
                send_sem=halo_send.at[side], recv_sem=halo_sem.at[side],
                device_id={"queue": to, "head": j}, device_id_type=MESH,
            )

        def forward(n, carry):
            for side in range(2):
                src = (1, GROUP)[side]
                wait_for(
                    kv.at[:, pl.ds(pl.multiple_of(src * slab + n * rows, rows), rows), :],
                    edge_sem.at[side, n],
                )
                halo(side, n).start()
            return carry

        lax.fori_loop(0, nz, forward, 0)
        for s in range(2):
            wait_for(kv.at[:, (s + 2) * slab : (s + 3) * slab, :], kv_sem.at[s])
        wait_for(meta, meta_sem)
        prompt_copy.wait()
        head_col = pl.multiple_of((j * PER + hl) * HD, HD)
        pk = [pkv.at[p, 0] for p in range(NPROMPT)]
        ones = jnp.ones((3 * slab, HD), jnp.bfloat16)
        within = jnp.where(j >= nz // 2, j - nz // 2, j)
        mine4 = 2 * arc + jnp.where(j >= nz // 2, 1, 0)
        toward = jnp.where(within >= nz // 4, 1, 3)

        def one_block(t, carry):
            turn = jnp.where(t >= 6, 3, jnp.where(t >= 4, 2, jnp.where(t >= 2, 1, 0)))
            quarter = wrapped(
                mine4
                + jnp.where(turn == 0, 2, jnp.where(turn == 1, toward, jnp.where(turn == 2, 4 - toward, 0))),
                4,
            )
            side = jnp.where(quarter >= 2, 1, 0)
            low = quarter - 2 * side
            s = wrapped(2 * side + t - 2 * turn - 1, GROUP)

            @pl.when(t == 0)
            def _():
                wait_for(kv.at[:, (GROUP + 1) * slab :, :], halo_sem.at[0])
                wait_for(kv.at[:, :slab, :], halo_sem.at[1])

            left_ok = (c > 0) | (s > 0)
            right_ok = (c < nq // GROUP - 1) | (s < GROUP - 1)
            here = meta[s]
            gate = jnp.where(
                hl == 0, here[4:5, :], jnp.where(hl == 1, here[5:6, :], here[6:7, :])
            )
            row = pl.multiple_of(s * slab + low * half, half)
            wait_for(qb.at[:, pl.ds(row, half), :], q_sem.at[s * 2 + low])
            qv = qb[0, pl.ds(row, half), :]
            first = pl.multiple_of(s * slab, slab)
            keys = kv[0, pl.ds(first, 3 * slab), :]
            values = kv[1, pl.ds(first, 3 * slab), :]
            scores = lax.dot_general(
                qv, keys, (((1,), (1,)), ((), ())), preferred_element_type=jnp.float32
            )
            parts = [scores[:, i * slab : (i + 1) * slab] for i in range(3)]
            tops = [jnp.max(x, axis=1, keepdims=True) for x in parts]
            top = jnp.maximum(
                tops[1],
                jnp.maximum(jnp.where(left_ok, tops[0], NEG), jnp.where(right_ok, tops[2], NEG)),
            )
            shifts = (jnp.where(left_ok, top, FAR), top, jnp.where(right_ok, top, FAR))
            probs = jnp.concatenate(
                [jnp.exp2((x - y) * SCALE).astype(jnp.bfloat16) for x, y in zip(parts, shifts)],
                axis=1,
            )
            both = jnp.dot(
                probs, jnp.concatenate([values, ones], axis=1),
                preferred_element_type=jnp.float32,
            )
            result = both[:, :HD] / both[:, HD:]

            chosen = jnp.concatenate(
                [
                    jnp.broadcast_to(
                        jnp.where(low == 0, here[i : i + 1, :], here[i + 2 : i + 3, :]), (128, 128)
                    ).T
                    for i in range(2)
                ],
                axis=0,
            )
            cross = jnp.zeros((half, L), jnp.float32)
            for p in range(NPROMPT):
                one = lax.dot_general(
                    qv, pk[p][...], (((1,), (1,)), ((), ())),
                    preferred_element_type=jnp.float32,
                )
                cross = jnp.where(chosen == float(p), one, cross)
            cross_top = jnp.max(cross, axis=1, keepdims=True)
            weights = jnp.exp2((cross - cross_top) * SCALE)
            total = jnp.sum(weights, axis=1, keepdims=True)
            masked = jnp.concatenate(
                [
                    jnp.where(chosen == float(p), weights, 0.0).astype(jnp.bfloat16)
                    for p in range(NPROMPT)
                ],
                axis=1,
            )
            stacked = jnp.concatenate([pkv[p, 1] for p in range(NPROMPT)], axis=0)
            result = result + jnp.dot(
                masked, stacked, preferred_element_type=jnp.float32
            ) / total
            ob[pl.ds(row, half), :] = (gate * result).astype(jnp.bfloat16)

            target = wrapped(base + s + 1, nq)
            for i in range(nz // 2):
                z2 = low * (nz // 2) + i
                src = ob.at[pl.ds(pl.multiple_of(row + i * rows, rows), rows), :]
                dst = out.at[:, pl.ds(head_col, HD)]
                mine = (target == q) & (j == z2)

                @pl.when(mine)
                def _():
                    pltpu.make_async_copy(src, dst, out_sem).start()

                @pl.when(jnp.logical_not(mine))
                def _():
                    pltpu.make_async_remote_copy(
                        src_ref=src, dst_ref=dst, send_sem=out_send, recv_sem=out_sem,
                        device_id={"queue": target, "head": z2}, device_id_type=MESH,
                    ).start()

            return carry

        lax.fori_loop(0, 2 * GROUP, one_block, 0)
        for side in range(2):
            wait_for(kv.at[:, :slab, :], halo_send.at[side])

        @pl.when(a == 0)
        def _():
            wait_for(ob, out_send)

        @pl.when(a > 0)
        def _():
            wait_for(ob.at[: GROUP * slab - rows, :], out_send)

    @pl.when(jnp.logical_not(works))
    def _():
        wait_for(meta, meta_sem)
        prompt_copy.wait()

    if not THROTTLE:
        sent(1, 3, kv_send)
    sent(0, 1, q_send)
    for i in range(GROUP - 1):
        wait_for(meta_src, meta_send.at[i])
    wait_for(out, out_sem)


def solution(mesh):
    nq, nz = mesh.shape["queue"], mesh.shape["head"]

    def per_device(
        projected, prompt_states, region_map, region_prompt, step_index, time_gates, incoming
    ):
        rows, _, channels = projected.shape
        slab = rows * nz
        anywhere = pl.BlockSpec(memory_space=pl.ANY)
        scalars = pl.BlockSpec(memory_space=pltpu.SMEM)
        dma = pltpu.SemaphoreType.DMA

        def kernel(*refs):
            attention_kernel(nq, nz, *refs)

        moved = pl.pallas_call(
            kernel,
            out_shape=jax.ShapeDtypeStruct((rows, channels), jnp.bfloat16),
            in_specs=[anywhere, anywhere, anywhere, scalars, scalars, anywhere],
            out_specs=anywhere,
            scratch_shapes=[
                pltpu.VMEM((2, (GROUP + 2) * slab, HD), jnp.bfloat16),
                pltpu.VMEM((1, GROUP * slab, HD), jnp.bfloat16),
                pltpu.VMEM((GROUP * slab, HD), jnp.bfloat16),
                pltpu.VMEM((NPROMPT, 2, L, HD), jnp.bfloat16),
                pltpu.VMEM(region_map.shape, jnp.int32),
                pltpu.VMEM(time_gates.shape, jnp.float32),
                pltpu.VMEM((8, 128), jnp.float32),
                pltpu.VMEM((GROUP, 8, 128), jnp.float32),
                dma((2, nz)),
                dma((2,)),
                dma((2 * GROUP,)),
                dma((2,)),
                dma,
                dma,
                dma((3,)),
                dma,
                dma,
                dma((2,)),
                dma((GROUP - 1,)),
                dma,
            ],
            compiler_params=pltpu.CompilerParams(
                collective_id=0, has_side_effects=True, vmem_limit_bytes=63_400_000
            ),
        )(
            projected.transpose(1, 0, 2), prompt_states, region_map, region_prompt, step_index,
            time_gates,
        )
        return jnp.where(lax.axis_index("queue") == 0, incoming, moved)

    return jax.shard_map(
        per_device,
        mesh=mesh,
        in_specs=(
            P(("queue", "head"), None, None),
            P(None, None, None, "head"),
            P("queue", None),
            P("queue", None),
            P("queue"),
            P(None, "head"),
            P("head", None),
        ),
        out_specs=P(("queue", "head"), None),
        check_vma=False,
    )
```

time: 113 us -> 99.2 us (0.88)
  Pallas kernels: 106 us -> 96.2 us
  local copies, waits for them, and re-layouts: 4.9 us -> 0.01 us
    pallas_call x1, Pallas kernels: 106 us -> 96.2 us  [per_device(): pl.pallas_call(kernel, out_shape=jax.ShapeDtypeStruct((rows, channels), j...]
    unnamed x12 -> x2, local copies, waits for them, and re-layouts: 4.9 us -> 0.01 us
where the time goes in v2:
time: 99.2 us; the launch traced here: 98.7 us
  Pallas kernels  96.2 us (97%)
  other arithmetic  1.81 us (2%)
    pallas_call x1, Pallas kernels, per_device(): pl.pallas_call(kernel, out_shape=jax.ShapeDtypeStruct((rows, channels), j...  96.2 us

profile of v2, /device:TPU:1, one launch (start us, length us, event | category | flops | bytes accessed | tf_op | source)
XLA Modules:
  0.0 98.7 jit_solution(12025404388432928730)
XLA Ops:
  0.7 0.0 copy-start
  0.7 96.2 %shard_map.73 = bf16[64,3072]{1,0:T(8,128)(2,1)} custom-call(bf16[3,64,3072]{2,1,0:T(8,128)(2,1)} %bitcast.1, bf16[8,2,128,384]{3,2,1,0:T(8,128)(2,1)} %refs_1_.1, s32[1,512]{1,0:T(1,128)} %refs_2_.1, s32[1,4]{1,0:T(1,128)} %refs_3_.1, s32[1]{0:T(128)S(6)} %copy.8.refs_4_, f32[50,384]{1,0:T(8,128)} %refs_5_.1), custom_call_target="tpu_custom_call" | custom-call | tf_op jit(solution)/shard_map/pallas_call | solution.py:378
  96.9 0.0 copy-done
  96.9 1.8 %broadcast_select_fusion = bf16[64,3072]{1,0:T(8,128)(2,1)} fusion(bf16[64,3072]{1,0:T(8,128)(2,1)S(1)} %copy-done, bf16[64,3072]{1,0:T(8,128)(2,1)} %shard_map.73, pred[]{:T(512)S(6)} %eq.3), kind=kLoop, calls=%fused_computation | loop fusion | flops 196608 | bytes 1179649 | tf_op jit(solution)/shard_map/jit(_where)/select_n | solution.py:412
Async XLA Ops:
  0.7 96.3 %copy-start = (bf16[64,3072]{1,0:T(8,128)(2,1)S(1)}, bf16[64,3072]{1,0:T(8,128)(2,1)}, u32[]{:S(2)}) copy-start(bf16[64,3072]{1,0:T(8,128)(2,1)} %param.13) | copy-start | bytes 1179652

commit v3 on v2

--- a/solution.py
+++ b/solution.py
@@ -18,13 +18,11 @@
 FAR = 1e30
 SCALE = math.log2(math.e) / math.sqrt(HD)
 THROTTLE = False
-FARKV = True
-FARQ = False
 MESH = pl.DeviceIdType.MESH
 
 
 def free_place(z):
-    upper = (z == 1) | (z == 2) | (z == 4) | (z == 7)
+    upper = (z == 1) | (z == 3) | (z == 4) | (z == 7)
     return jnp.where(upper, 3, 1)
 
 
@@ -41,7 +39,7 @@
     proj, prompts, rmap, rprompt, step, gates,
     out,
     kv, qb, ob, pkv, rmap_v, gates_v, meta_src, meta,
-    edge_sem, kv_sem, q_sem, halo_sem, meta_sem, out_sem, local_sem,
+    kv_sem, ready, q_sem, halo_sem, meta_sem, out_sem, local_sem,
     kv_send, q_send, halo_send, meta_send, out_send,
 ):
     rows = proj.shape[1]
@@ -60,8 +58,9 @@
     free = free_place(j)
     works = a != free
     hl = a - jnp.where(a > free, 1, 0)
-    right = wrapped(q + GROUP, nq)
-    left = wrapped(q - GROUP, nq)
+    has_left = c > 0
+    has_right = q + GROUP < nq
+    sides = ((has_left, q - GROUP), (has_right, q + GROUP))
 
     barrier = pltpu.get_barrier_semaphore()
 
@@ -73,18 +72,19 @@
             device_id_type=MESH,
         )
 
-    def greet_chip(m, carry):
-        chip = wrapped(z + m, ring)
+    for off in (1, -1):
+        chip = wrapped(z + off, ring)
         greet(chip, 0)
         greet(chip, 1)
-        return carry
-
-    lax.fori_loop(1, ring, greet_chip, 0)
     greet(z, 1 - core)
-    for side in (left, right):
-        pl.semaphore_signal(
-            barrier, inc=1, device_id={"queue": side, "head": j}, device_id_type=MESH
-        )
+    for there, other in sides:
+
+        @pl.when(there)
+        def _():
+            pl.semaphore_signal(
+                barrier, inc=1, device_id={"queue": other, "head": j}, device_id_type=MESH
+            )
+
     map_copy = pltpu.make_async_copy(rmap, rmap_v, local_sem.at[0])
     gate_copy = pltpu.make_async_copy(gates, gates_v, local_sem.at[1])
     lane = pl.multiple_of(jnp.minimum(hl, PER - 1) * HD, HD)
@@ -94,9 +94,37 @@
     map_copy.start()
     gate_copy.start()
     prompt_copy.start()
-    pl.semaphore_wait(barrier, 2 * ring + 1)
-
-    def spread(first, last, dst, send_sem, recv_sem, far):
+    both_sides = has_left & has_right
+
+    @pl.when(both_sides)
+    def _():
+        pl.semaphore_wait(barrier, 7)
+
+    @pl.when(jnp.logical_not(both_sides))
+    def _():
+        pl.semaphore_wait(barrier, 6)
+
+    for there, slot in ((has_left, 0), (has_right, GROUP + 1)):
+
+        @pl.when(jnp.logical_not(there))
+        def _():
+            kv[:, slot * slab : (slot + 1) * slab, :] = jnp.zeros((2, slab, HD), jnp.bfloat16)
+
+
+    def tell(n):
+        for off in (2**n, -(2**n)):
+            chip = wrapped(z + off, ring)
+            upper = jnp.where(chip >= nz, 1, 0)
+            pl.semaphore_signal(
+                ready.at[n], inc=1,
+                device_id={"queue": base + 2 * upper + core, "head": chip - nz * upper},
+                device_id_type=MESH,
+            )
+
+    rounds = nz.bit_length() - 1
+    tell(0)
+
+    def spread(first, last, dst, send_sem, recv_sem, opening):
         def piece(chip, k):
             upper = jnp.where(chip >= nz, 1, 0)
             z2 = chip - nz * upper
@@ -121,8 +149,7 @@
                 pl.when(real)(go)
 
         def both_ways(m, carry):
-            d = nz - m if far else m
-            for off in (d, -d):
+            for off in (m, -m):
                 chip = wrapped(z + off, ring)
                 send(chip, 0)
                 send(chip, 1)
@@ -141,14 +168,18 @@
                     device_id={"queue": q2, "head": z2}, device_id_type=MESH,
                 ).start()
 
+        if opening:
+            for n in range(rounds):
+                lax.fori_loop(2**n // 2 + 1, 2**n + 1, both_ways, 0)
+                pl.semaphore_wait(ready.at[n], 2)
+                if n + 1 < rounds:
+                    tell(n + 1)
+            lax.fori_loop(nz // 2 + 1, nz, both_ways, 0)
+        else:
+            lax.fori_loop(1, nz, both_ways, 0)
         opposite = wrapped(z + nz, ring)
-        if far:
-            send(opposite, 0)
-            send(opposite, 1)
-        lax.fori_loop(1, nz, both_ways, 0)
-        if not far:
-            send(opposite, 0)
-            send(opposite, 1)
+        send(opposite, 0)
+        send(opposite, 1)
 
     def sent(first, last, sem):
         @pl.when(works)
@@ -161,15 +192,7 @@
 
     kv_row = pl.multiple_of((a + 1) * slab + j * rows, rows)
     kv_dst = kv.at[:, pl.ds(kv_row, rows), :]
-    at_edge = (a == 0) | (a == GROUP - 1)
-
-    @pl.when(at_edge)
-    def _():
-        spread(1, 3, kv_dst, kv_send, edge_sem.at[jnp.where(a == 0, 0, 1), j], FARKV)
-
-    @pl.when(jnp.logical_not(at_edge))
-    def _():
-        spread(1, 3, kv_dst, kv_send, kv_sem.at[core], FARKV)
+    spread(1, 3, kv_dst, kv_send, kv_sem.at[a, j], True)
 
     map_copy.wait()
     gate_copy.wait()
@@ -199,13 +222,13 @@
     q_row = pl.multiple_of(a * slab + j * rows, rows)
     spread(
         0, 1, qb.at[:, pl.ds(q_row, rows), :], q_send,
-        q_sem.at[a * 2 + jnp.where(j >= nz // 2, 1, 0)], FARQ,
+        q_sem.at[a * 2 + jnp.where(j >= nz // 2, 1, 0)], False,
     )
 
     @pl.when(works)
     def _():
         def halo(side, n):
-            src, dst, to = ((1, GROUP + 1, left), (GROUP, 0, right))[side]
+            src, dst, to = ((1, GROUP + 1, q - GROUP), (GROUP, 0, q + GROUP))[side]
             return pltpu.make_async_remote_copy(
                 src_ref=kv.at[:, pl.ds(pl.multiple_of(src * slab + n * rows, rows), rows), :],
                 dst_ref=kv.at[:, pl.ds(pl.multiple_of(dst * slab + n * rows, rows), rows), :],
@@ -218,14 +241,22 @@
                 src = (1, GROUP)[side]
                 wait_for(
                     kv.at[:, pl.ds(pl.multiple_of(src * slab + n * rows, rows), rows), :],
-                    edge_sem.at[side, n],
+                    kv_sem.at[src - 1, n],
                 )
-                halo(side, n).start()
+
+
+                @pl.when(sides[side][0])
+                def _():
+                    halo(side, n).start()
+
+            for s in range(1, GROUP - 1):
+                wait_for(
+                    kv.at[:, pl.ds(pl.multiple_of((s + 1) * slab + n * rows, rows), rows), :],
+                    kv_sem.at[s, n],
+                )
             return carry
 
         lax.fori_loop(0, nz, forward, 0)
-        for s in range(2):
-            wait_for(kv.at[:, (s + 2) * slab : (s + 3) * slab, :], kv_sem.at[s])
         wait_for(meta, meta_sem)
         prompt_copy.wait()
         head_col = pl.multiple_of((j * PER + hl) * HD, HD)
@@ -248,11 +279,17 @@
 
             @pl.when(t == 0)
             def _():
-                wait_for(kv.at[:, (GROUP + 1) * slab :, :], halo_sem.at[0])
-                wait_for(kv.at[:, :slab, :], halo_sem.at[1])
-
-            left_ok = (c > 0) | (s > 0)
-            right_ok = (c < nq // GROUP - 1) | (s < GROUP - 1)
+                @pl.when(has_right)
+                def _():
+                    wait_for(kv.at[:, (GROUP + 1) * slab :, :], halo_sem.at[0])
+
+                @pl.when(has_left)
+                def _():
+                    wait_for(kv.at[:, :slab, :], halo_sem.at[1])
+
+
+            left_ok = has_left | (s > 0)
+            right_ok = has_right | (s < GROUP - 1)
             here = meta[s]
             gate = jnp.where(
                 hl == 0, here[4:5, :], jnp.where(hl == 1, here[5:6, :], here[6:7, :])
@@ -315,7 +352,7 @@
             ) / total
             ob[pl.ds(row, half), :] = (gate * result).astype(jnp.bfloat16)
 
-            target = wrapped(base + s + 1, nq)
+            target = base + s + 1
             for i in range(nz // 2):
                 z2 = low * (nz // 2) + i
                 src = ob.at[pl.ds(pl.multiple_of(row + i * rows, rows), rows), :]
@@ -326,7 +363,7 @@
                 def _():
                     pltpu.make_async_copy(src, dst, out_sem).start()
 
-                @pl.when(jnp.logical_not(mine))
+                @pl.when(jnp.logical_not(mine) & (target < nq))
                 def _():
                     pltpu.make_async_remote_copy(
                         src_ref=src, dst_ref=dst, send_sem=out_send, recv_sem=out_sem,
@@ -337,15 +374,20 @@
 
         lax.fori_loop(0, 2 * GROUP, one_block, 0)
         for side in range(2):
-            wait_for(kv.at[:, :slab, :], halo_send.at[side])
-
-        @pl.when(a == 0)
-        def _():
-            wait_for(ob, out_send)
-
-        @pl.when(a > 0)
-        def _():
-            wait_for(ob.at[: GROUP * slab - rows, :], out_send)
+
+            @pl.when(sides[side][0])
+            def _():
+                wait_for(kv.at[:, :slab, :], halo_send.at[side])
+
+        for slabs, there in ((GROUP, has_right), (GROUP - 1, jnp.logical_not(has_right))):
+
+            @pl.when(there & (a == 0))
+            def _():
+                wait_for(ob.at[: slabs * slab, :], out_send)
+
+            @pl.when(there & (a > 0))
+            def _():
+                wait_for(ob.at[: slabs * slab - rows, :], out_send)
 
     @pl.when(jnp.logical_not(works))
     def _():
@@ -357,7 +399,10 @@
     sent(0, 1, q_send)
     for i in range(GROUP - 1):
         wait_for(meta_src, meta_send.at[i])
-    wait_for(out, out_sem)
+
+    @pl.when(q > 0)
+    def _():
+        wait_for(out, out_sem)
 
 
 def solution(mesh):
@@ -389,8 +434,8 @@
                 pltpu.VMEM(time_gates.shape, jnp.float32),
                 pltpu.VMEM((8, 128), jnp.float32),
                 pltpu.VMEM((GROUP, 8, 128), jnp.float32),
-                dma((2, nz)),
-                dma((2,)),
+                dma((GROUP, nz)),
+                pltpu.SemaphoreType.REGULAR((3,)),
                 dma((2 * GROUP,)),
                 dma((2,)),
                 dma,

time: 99.2 us -> 97.2 us (0.980); the launches traced: 98.7 us -> 95.7 us
  Pallas kernels: 96.2 us -> 93.2 us
    pallas_call x1, Pallas kernels: 96.2 us -> 93.2 us  [per_device(): pl.pallas_call(kernel, out_shape=jax.ShapeDtypeStruct((rows, channels), j...]
where the time goes in v3:
time: 97.2 us; the launch traced here: 95.7 us
  Pallas kernels  93.2 us (96%)
  other arithmetic  1.81 us (2%)
    pallas_call x1, Pallas kernels, per_device(): pl.pallas_call(kernel, out_shape=jax.ShapeDtypeStruct((rows, channels), j...  93.2 us

profile of v3, /device:TPU:1, one launch (start us, length us, event | category | flops | bytes accessed | tf_op | source)
XLA Modules:
  0.0 95.7 jit_solution(18056977837689610233)
XLA Ops:
  0.7 0.0 copy-start
  0.7 93.2 %shard_map.73 = bf16[64,3072]{1,0:T(8,128)(2,1)} custom-call(bf16[3,64,3072]{2,1,0:T(8,128)(2,1)} %bitcast.1, bf16[8,2,128,384]{3,2,1,0:T(8,128)(2,1)} %refs_1_.1, s32[1,512]{1,0:T(1,128)} %refs_2_.1, s32[1,4]{1,0:T(1,128)} %refs_3_.1, s32[1]{0:T(128)S(6)} %copy.8.refs_4_, f32[50,384]{1,0:T(8,128)} %refs_5_.1), custom_call_target="tpu_custom_call" | custom-call | tf_op jit(solution)/shard_map/pallas_call | solution.py:423
  93.9 0.0 copy-done
  93.9 1.8 %broadcast_select_fusion = bf16[64,3072]{1,0:T(8,128)(2,1)} fusion(bf16[64,3072]{1,0:T(8,128)(2,1)S(1)} %copy-done, bf16[64,3072]{1,0:T(8,128)(2,1)} %shard_map.73, pred[]{:T(512)S(6)} %eq.3), kind=kLoop, calls=%fused_computation | loop fusion | flops 196608 | bytes 1179649 | tf_op jit(solution)/shard_map/jit(_where)/select_n | solution.py:457
Async XLA Ops:
  0.7 93.2 %copy-start = (bf16[64,3072]{1,0:T(8,128)(2,1)S(1)}, bf16[64,3072]{1,0:T(8,128)(2,1)}, u32[]{:S(2)}) copy-start(bf16[64,3072]{1,0:T(8,128)(2,1)} %param.13) | copy-start | bytes 1179652

commit v4 on v3

--- a/solution.py
+++ b/solution.py
@@ -264,15 +264,16 @@
         ones = jnp.ones((3 * slab, HD), jnp.bfloat16)
         within = jnp.where(j >= nz // 2, j - nz // 2, j)
         mine4 = 2 * arc + jnp.where(j >= nz // 2, 1, 0)
-        toward = jnp.where(within >= nz // 4, 1, 3)
 
         def one_block(t, carry):
             turn = jnp.where(t >= 6, 3, jnp.where(t >= 4, 2, jnp.where(t >= 2, 1, 0)))
-            quarter = wrapped(
-                mine4
-                + jnp.where(turn == 0, 2, jnp.where(turn == 1, toward, jnp.where(turn == 2, 4 - toward, 0))),
-                4,
-            )
+            targets = (
+                jnp.where(mine4 == 0, 0, jnp.where(mine4 == 1, 3, jnp.where(mine4 == 2, 0, 0))),
+                jnp.where(mine4 == 0, 2, jnp.where(mine4 == 1, 0, jnp.where(mine4 == 2, 3, 2))),
+                jnp.where(mine4 == 0, 3, jnp.where(mine4 == 1, 2, jnp.where(mine4 == 2, 1, 1))),
+                jnp.where(mine4 == 0, 1, jnp.where(mine4 == 1, 1, jnp.where(mine4 == 2, 2, 3))),
+            )
+            quarter = jnp.where(turn == 0, targets[0], jnp.where(turn == 1, targets[1], jnp.where(turn == 2, targets[2], targets[3])))
             side = jnp.where(quarter >= 2, 1, 0)
             low = quarter - 2 * side
             s = wrapped(2 * side + t - 2 * turn - 1, GROUP)

time: 97.2 us -> 95 us (0.977)
  the two profiles are of different devices: /device:TPU:1 before, /device:TPU:39 now
where the time goes in v4:
time: 95 us; the launch traced here: 94.8 us
  Pallas kernels  92.3 us (97%)
  other arithmetic  1.81 us (2%)
    pallas_call x1, Pallas kernels, per_device(): pl.pallas_call(kernel, out_shape=jax.ShapeDtypeStruct((rows, channels), j...  92.3 us

profile of v4, /device:TPU:39, one launch (start us, length us, event | category | flops | bytes accessed | tf_op | source)
XLA Modules:
  0.0 94.8 jit_solution(14878658866341447712)
XLA Ops:
  0.7 0.0 copy-start
  0.7 92.3 %shard_map.73 = bf16[64,3072]{1,0:T(8,128)(2,1)} custom-call(bf16[3,64,3072]{2,1,0:T(8,128)(2,1)} %bitcast.1, bf16[8,2,128,384]{3,2,1,0:T(8,128)(2,1)} %refs_1_.1, s32[1,512]{1,0:T(1,128)} %refs_2_.1, s32[1,4]{1,0:T(1,128)} %refs_3_.1, s32[1]{0:T(128)S(6)} %copy.8.refs_4_, f32[50,384]{1,0:T(8,128)} %refs_5_.1), custom_call_target="tpu_custom_call" | custom-call | tf_op jit(solution)/shard_map/pallas_call | solution.py:424
  93.0 0.0 copy-done
  93.0 1.8 %broadcast_select_fusion = bf16[64,3072]{1,0:T(8,128)(2,1)} fusion(bf16[64,3072]{1,0:T(8,128)(2,1)S(1)} %copy-done, bf16[64,3072]{1,0:T(8,128)(2,1)} %shard_map.73, pred[]{:T(512)S(6)} %eq.3), kind=kLoop, calls=%fused_computation | loop fusion | flops 196608 | bytes 1179649 | tf_op jit(solution)/shard_map/jit(_where)/select_n | solution.py:458
Async XLA Ops:
  0.7 92.4 %copy-start = (bf16[64,3072]{1,0:T(8,128)(2,1)S(1)}, bf16[64,3072]{1,0:T(8,128)(2,1)}, u32[]{:S(2)}) copy-start(bf16[64,3072]{1,0:T(8,128)(2,1)} %param.13) | copy-start | bytes 1179652

commit v5 on v4

--- a/solution.py
+++ b/solution.py
@@ -176,7 +176,7 @@
                     tell(n + 1)
             lax.fori_loop(nz // 2 + 1, nz, both_ways, 0)
         else:
-            lax.fori_loop(1, nz, both_ways, 0)
+            lax.fori_loop(1, nz, lambda m, carry: both_ways(nz - m, carry), 0)
         opposite = wrapped(z + nz, ring)
         send(opposite, 0)
         send(opposite, 1)

time: 95 us -> 93 us (0.979)
  the two profiles are of different devices: /device:TPU:39 before, /device:TPU:1 now
where the time goes in v5:
time: 93 us; the launch traced here: 92.1 us
  Pallas kernels  89.6 us (96%)
  other arithmetic  1.81 us (2%)
    pallas_call x1, Pallas kernels, per_device(): pl.pallas_call(kernel, out_shape=jax.ShapeDtypeStruct((rows, channels), j...  89.6 us

profile of v5, /device:TPU:1, one launch (start us, length us, event | category | flops | bytes accessed | tf_op | source)
XLA Modules:
  0.0 92.1 jit_solution(1275115426040893094)
XLA Ops:
  0.7 0.0 copy-start
  0.7 89.6 %shard_map.73 = bf16[64,3072]{1,0:T(8,128)(2,1)} custom-call(bf16[3,64,3072]{2,1,0:T(8,128)(2,1)} %bitcast.1, bf16[8,2,128,384]{3,2,1,0:T(8,128)(2,1)} %refs_1_.1, s32[1,512]{1,0:T(1,128)} %refs_2_.1, s32[1,4]{1,0:T(1,128)} %refs_3_.1, s32[1]{0:T(128)S(6)} %copy.8.refs_4_, f32[50,384]{1,0:T(8,128)} %refs_5_.1), custom_call_target="tpu_custom_call" | custom-call | tf_op jit(solution)/shard_map/pallas_call | solution.py:424
  90.2 0.0 copy-done
  90.2 1.8 %broadcast_select_fusion = bf16[64,3072]{1,0:T(8,128)(2,1)} fusion(bf16[64,3072]{1,0:T(8,128)(2,1)S(1)} %copy-done, bf16[64,3072]{1,0:T(8,128)(2,1)} %shard_map.73, pred[]{:T(512)S(6)} %eq.3), kind=kLoop, calls=%fused_computation | loop fusion | flops 196608 | bytes 1179649 | tf_op jit(solution)/shard_map/jit(_where)/select_n | solution.py:458
Async XLA Ops:
  0.7 89.6 %copy-start = (bf16[64,3072]{1,0:T(8,128)(2,1)S(1)}, bf16[64,3072]{1,0:T(8,128)(2,1)}, u32[]{:S(2)}) copy-start(bf16[64,3072]{1,0:T(8,128)(2,1)} %param.13) | copy-start | bytes 1179652
